TPU v7x, 256 devices: a whole 4x4x8 slice. The times are simulated.
256 devices in a mesh: row: 16 (over z_lo, y, core), col: 16 (over x, z_hi).
Axes of the slice: x: 4, y: 4, z: 8 (z_hi: 4, z_lo: 2; z = z_hi * 2 + z_lo), core: 2. Of those that a mesh axis runs over, the one named last changes fastest.
Arguments:
- tile_values: bfloat16 [16, 16, 320, 128, 128], P('row', 'col')
- tile_rows: int32 [16, 16, 320], P('row', 'col'), may hold values from 0 to 511
- tile_cols: int32 [16, 16, 320], P('row', 'col'), may hold values from 0 to 255
- tile_counts: int32 [16, 16], P('row', 'col'), may hold values from 160 to 320, as said below
- solution: float32 [4, 524288], P(None, ('col', 'row')), may hold values from -6 to 6
- residual: float32 [4, 1048576], P(None, ('row', 'col')), may hold values from -6 to 6
- direction: float32 [4, 524288], P(None, ('col', 'row')), may hold values from -6 to 6
- grad_norm: float32 [4], replicated, may hold values from 314572.8 to 3145728
Outputs:
- new_solution: float32 [4, 524288], P(None, ('col', 'row'))
- new_residual: float32 [4, 1048576], P(None, ('row', 'col'))
- new_direction: float32 [4, 524288], P(None, ('col', 'row'))
Inputs may be any that keep to these rules, and one draw needn't show every extreme that they name: Each device uses its first tile_counts slots; at least half of 320, and some device uses all 320.
All inputs are finite; a program needn't handle non-finite values.
Results may differ from a plain program's by a relative error of at most 0.0032.
Values may be sent and summed in bfloat16 or wider, within the bound.
A program may use at most 128 MiB of HBM per device.

v0:
```python
import jax
import jax.numpy as jnp
from jax import lax
from jax.sharding import PartitionSpec as P

BR = 512
BC = 256


def local_product(
    tile_data, slot_rows, slot_cols, slot_used, vector_group, blocks_out, transpose_dir
):
    tile_edge = tile_data.shape[-1]
    rhs_total = vector_group.shape[0]
    blocks = vector_group.reshape(rhs_total, -1, tile_edge)
    if transpose_dir:
        picked = blocks[:, slot_rows, :]
        contrib = jnp.einsum("kab,rka->krb", tile_data, picked, preferred_element_type=jnp.float32)
        target = slot_cols
    else:
        picked = blocks[:, slot_cols, :]
        contrib = jnp.einsum("kab,rkb->kra", tile_data, picked, preferred_element_type=jnp.float32)
        target = slot_rows
    contrib = contrib * slot_used[:, None, None]
    summed = jax.ops.segment_sum(contrib, target, num_segments=blocks_out)
    return jnp.moveaxis(summed, 0, 1).reshape(rhs_total, blocks_out * tile_edge)


def on_device(
    tile_values, tile_rows, tile_cols, tile_counts, solution, residual, direction, grad_norm
):
    slot_total = tile_values.shape[2]
    tile_data = tile_values[0, 0]
    slot_rows = tile_rows[0, 0]
    slot_cols = tile_cols[0, 0]
    slot_used = (jnp.arange(slot_total, dtype=jnp.int32) < tile_counts[0, 0]).astype(jnp.float32)
    direction_low = direction.astype(jnp.bfloat16)
    direction_group = lax.all_gather(direction_low, "row", axis=1, tiled=True)
    image_part = local_product(
        tile_data, slot_rows, slot_cols, slot_used, direction_group, BR, False
    )
    image_piece = lax.psum_scatter(image_part, "col", scatter_dimension=1, tiled=True)
    curvature = lax.psum(jnp.sum(image_piece * image_piece, axis=1), ("row", "col"))
    step_len = grad_norm / curvature
    new_residual = residual - step_len[:, None] * image_piece
    residual_low = lax.all_gather(new_residual.astype(jnp.bfloat16), "col", axis=1, tiled=True)
    new_solution = solution + step_len[:, None] * direction
    gradient_part = local_product(
        tile_data, slot_rows, slot_cols, slot_used, residual_low, BC, True
    )
    gradient = lax.psum_scatter(gradient_part, "row", scatter_dimension=1, tiled=True)
    norm_next = lax.psum(jnp.sum(gradient * gradient, axis=1), ("row", "col"))
    beta_ratio = norm_next / grad_norm
    new_direction = gradient + beta_ratio[:, None] * direction
    return (new_solution, new_residual, new_direction)


def solution(mesh):
    in_specs = (
        P("row", "col", None, None, None),
        P("row", "col", None),
        P("row", "col", None),
        P("row", "col"),
        P(None, ("col", "row")),
        P(None, ("row", "col")),
        P(None, ("col", "row")),
        P(),
    )
    out_specs = (P(None, ("col", "row")), P(None, ("row", "col")), P(None, ("col", "row")))
    return jax.shard_map(
        on_device, mesh=mesh, in_specs=in_specs, out_specs=out_specs, check_vma=False
    )
```

profile of v0, /device:TPU:1, one launch (start us, length us, event | category | flops | bytes accessed | tf_op | source)
XLA Modules:
  0.0 784.3 jit_solution(5543374480649377287)
XLA Ops:
  7.9 0.8 convert_element_type.13
  8.6 22.3 %all_gather.6 = bf16[4,32768]{1,0:T(4,128)(2,1)S(1)} all-gather(bf16[4,2048]{1,0:T(4,128)(2,1)S(1)} %convert_element_type.13), channel_id=1, replica_groups=mesh['row'=16,'col'=16] {'row'}, dimensions={1}, use_global_device_ids=true | all-gather | bytes 278528 | tf_op jit(solution)/shard_map/all_gather | solution.py:38
  30.9 0.7 fusion.13
  31.7 2.0 gather_fusion
  33.7 0.7 reduce
  34.4 8.1 %fusion.4 = f32[320,4,128]{2,1,0:T(4,128)S(1)} fusion(bf16[1,1,320,128,128]{4,3,2,1,0:T(8,128)(2,1)} %param.8, bf16[320,4,128]{2,1,0:T(4,128)(2,1)S(1)} %gather_fusion, f32[320]{0:T(512)S(1)} %fusion.12), kind=kOutput, calls=%fused_computation.8 | convolution fusion | flops 42106880 | bytes 11470080 | tf_op jit(solution)/shard_map/kab,rkb->kra/dot_general | solution.py:22
  42.5 0.2 broadcast_in_dim.4
  42.6 11.9 %scatter_fusion = f32[512,4,128]{2,1,0:T(4,128)S(1)} fusion(f32[512,4,128]{2,1,0:T(4,128)S(1)} %broadcast_in_dim.4, s32[320]{0:T(512)S(1)} %reduce, f32[320,4,128]{2,1,0:T(4,128)S(1)} %fusion.4), kind=kCustom, calls=%fused_computation.2 | custom fusion | flops 163840 | bytes 1967360 | tf_op jit(solution)/shard_map/scatter-add | solution.py:25
  54.6 16.1 %copy.11 = f32[4,65536]{0,1:T(8,128)} copy(f32[4,65536]{1,0:T(4,128)S(1)} %bitcast.35) | data formatting | bytes 2097152
  70.7 0.6 copy-done.3
  71.4 380.7 %reduce-scatter.7.cloned.1.call-done = f32[4096,4]{1,0:T(8,128)} async-done(((f32[65536,4]{1,0:T(8,128)}), f32[4096,4]{1,0:T(8,128)}) %reduce-scatter.7.cloned.1.call-update) | async-done | bytes 65552
  452.1 2.2 copy.12
  454.3 0.2 multiply_reduce_fusion
  454.4 77.2 %psum.14 = f32[4]{0:T(128)S(1)} all-reduce(f32[4]{0:T(128)S(1)} %multiply_reduce_fusion), channel_id=1, replica_groups=mesh['row'=16,'col'=16] {'row','col'}, use_global_device_ids=true, to_apply=%region_3.0 | all-reduce | flops 4 | bytes 32 | tf_op jit(solution)/shard_map/psum | solution.py:43
  531.7 0.7 fusion.15
  532.4 35.9 %all_gather.7 = bf16[4,65536]{1,0:T(4,128)(2,1)S(1)} all-gather(bf16[4,4096]{1,0:T(4,128)(2,1)S(1)} %get-tuple-element.3), channel_id=1, replica_groups=mesh['row'=16,'col'=16] {'col'}, dimensions={1}, use_global_device_ids=true | all-gather | bytes 557056 | tf_op jit(solution)/shard_map/all_gather | solution.py:46
  568.3 2.0 gather_fusion.1
  570.3 5.5 fusion.7
  576.0 12.0 %scatter_fusion.1 = f32[256,4,128]{2,1,0:T(4,128)S(1)} fusion(f32[256,4,128]{2,1,0:T(4,128)S(1)} %broadcast_in_dim.5, s32[320]{0:T(512)S(1)} %reduce.2, f32[320,4,128]{2,1,0:T(4,128)S(1)} %fusion.7), kind=kCustom, calls=%fused_computation.3 | custom fusion | flops 163840 | bytes 1967360 | tf_op jit(solution)/shard_map/scatter-add | solution.py:25
  587.9 8.6 %copy.13 = f32[4,32768]{0,1:T(8,128)} copy(f32[4,32768]{1,0:T(4,128)S(1)} %bitcast.36) | data formatting | bytes 1048576
  596.5 101.2 %reduce-scatter.9.cloned.1.call-done = f32[2048,4]{1,0:T(8,128)} async-done(((f32[32768,4]{1,0:T(8,128)}), f32[2048,4]{1,0:T(8,128)}) %reduce-scatter.9.cloned.1.call-update) | async-done | bytes 32784
  697.7 1.6 copy.14
  699.4 77.4 %psum.15 = f32[4]{0:T(128)S(1)} all-reduce(f32[4]{0:T(128)S(1)} %multiply_reduce_fusion.1), channel_id=1, replica_groups=mesh['row'=16,'col'=16] {'row','col'}, use_global_device_ids=true, to_apply=%region_7.0 | all-reduce | flops 4 | bytes 32 | tf_op jit(solution)/shard_map/psum | solution.py:52
  776.8 0.7 multiply_add_fusion
  (24 shorter events, 0.4 us)
Async XLA Ops:
  7.2 444.9 %reduce-scatter.7.cloned.1.call-start = ((), (), s32[]{:S(2)}) async-start(), calls=%async_computation.2 | async-start | bytes 35651584
  70.7 0.7 copy-start.3
  70.7 383.8 %copy-start.4 = (s32[1,1,320]{2,1,0:T(1,128)S(1)}, s32[1,1,320]{2,1,0:T(1,128)}, u32[]{:S(2)}) copy-start(s32[1,1,320]{2,1,0:T(1,128)} %param.10) | copy-start | bytes 3844
  70.7 461.0 %copy-start.5 = (f32[4]{0:T(128)S(1)}, f32[4]{0:T(128)}, u32[]{:S(2)}) copy-start(f32[4]{0:T(128)} %param.15) | copy-start | bytes 52
  70.7 461.0 %copy-start.1 = (f32[4,4096]{1,0:T(4,128)S(1)}, f32[4,4096]{1,0:T(4,128)}, u32[]{:S(2)}) copy-start(f32[4,4096]{1,0:T(4,128)} %param.13) | copy-start | bytes 196612
  70.7 627.0 %reduce-scatter.9.cloned.1.call-start = ((), (), s32[]{:S(2)}) async-start(), calls=%async_computation.3 | async-start | bytes 17825792
  596.5 180.3 %copy-start = (f32[4,2048]{1,0:T(4,128)S(1)}, f32[4,2048]{1,0:T(4,128)}, u32[]{:S(2)}) copy-start(f32[4,2048]{1,0:T(4,128)} %param.14) | copy-start | bytes 98308
  596.5 180.3 %copy-start.2 = (f32[4,2048]{1,0:T(4,128)S(1)}, f32[4,2048]{1,0:T(4,128)}, u32[]{:S(2)}) copy-start(f32[4,2048]{1,0:T(4,128)} %param.12) | copy-start | bytes 98308
Sparse Core Ops, SparseCore 0:
  70.8 381.1 reduce-scatter.6
  596.6 100.9 reduce-scatter.8
where the time goes:
time: 784 us
  waiting for transfers between devices  482 us (61%)
  blocking collectives  213 us (27%)
  local copies, waits for them, and re-layouts  33.2 us (4%)
  other arithmetic  27.9 us (4%)
  between operations  14.8 us (2%)
  matrix products  13.6 us (2%)
    unnamed x4, waiting for transfers between devices  482 us
    psum x1, blocking collectives, on_device(): norm_next = lax.psum(jnp.sum(gradient * gradient, axis=1), ('row', 'col'))  77.4 us
    psum x1, blocking collectives, on_device(): lax.psum(jnp.sum(image_piece * image_piece, axis=1), ('row', 'col'))  77.2 us
    all_gather x1, blocking collectives, on_device(): lax.all_gather(new_residual.astype(jnp.bfloat16), 'col', axis=1, tiled=True)  35.9 us
    unnamed x16, local copies, waits for them, and re-layouts  29 us
    scatter-add x2, other arithmetic, local_product(): summed = jax.ops.segment_sum(contrib, target, num_segments=blocks_out)  23.9 us
    all_gather x1, blocking collectives, on_device(): direction_group = lax.all_gather(direction_low, 'row', axis=1, tiled=True)  22.3 us
  transfers between devices with their start and end apart: 2, of which 2 were waited for; matrix products, arithmetic and copies ran while one was open for 0% of the time, Pallas kernels for 0%

commit v1 on v0

v1 whole, which is shorter than its diff:
```python
import jax
import jax.numpy as jnp
from jax import lax
from jax.experimental import pallas as pl
from jax.experimental.pallas import tpu as pltpu
from jax.sharding import PartitionSpec as P

TB = 128
RHS = 4
BR = 512
BC = 256
K = 320
HALF = K // 2
KPAD = 384
NG = 16
NX = 4
NZ = 4
PR = BR // NG
PC = BC // NG
F32 = jnp.float32
BF16 = jnp.bfloat16
MESH = pl.DeviceIdType.MESH


def remote(src, dst, send_sem, recv_sem, device):
    return pltpu.make_async_remote_copy(
        src_ref=src,
        dst_ref=dst,
        send_sem=send_sem,
        recv_sem=recv_sem,
        device_id=device,
        device_id_type=MESH,
    )


def turn(base, step, size):
    return lax.rem(base + step + size, size)


def repeat(count, body, unroll=1):
    def step(index, carry):
        body(index)
        return carry

    lax.fori_loop(0, count, step, 0, unroll=unroll)


def kernel(
    count_s, rows_s, cols_s, gamma_s, rows_v, cols_v, tiles, sol, res, dirn,
    out_sol, out_res, out_dir,
    t, xg, ag, rg, sb, r1, r2, gs, gr, dpiece, rpiece, image, xf, rf, ys, hilo, hit_r, hit_c,
    grad_r, idx, ca, cb, na, nb,
    t_sem, x_ss, x_rs, rz_ss, rz_rs, rx_ss, rx_rs, s1_ss, s1_rs, s2_ss, s2_rs,
    az_ss, az_rs, ax_ss, ax_rs, g_ss, g_rs, ca_ss, ca_rs, cb_ss, cb_rs, na_ss, na_rs, nb_ss, nb_rs,
):
    i = lax.axis_index("row")
    j = lax.axis_index("col")
    x = j // NZ
    z = lax.rem(j, NZ)

    def row_peer(d):
        return (turn(i, d, NG), j)

    def col_peer(d):
        return (i, turn(j, d, NG))

    def x_peer(d):
        return (i, turn(x, d, NX) * NZ + z)

    def z_peer(d):
        return (i, x * NZ + turn(z, d, NZ))

    def tile_copy(c):
        part = pl.ds(c * (K // 4), K // 4)
        return pltpu.make_async_copy(tiles.at[0, 0, part], t.at[part], t_sem.at[c])

    for c in range(4):
        tile_copy(c).start()

    for buf in (ca, cb, na, nb):
        buf[...] = jnp.zeros_like(buf)

    barrier = pltpu.get_barrier_semaphore()

    def greet(d):
        pl.semaphore_signal(barrier, inc=1, device_id=row_peer(d + 1), device_id_type=MESH)
        pl.semaphore_signal(barrier, inc=1, device_id=col_peer(d + 1), device_id_type=MESH)

    repeat(NG - 1, greet)

    def cut_dir(b):
        for r in range(RHS):
            dpiece[r, pl.ds(b, 1), :] = dirn[pl.ds(r, 1), pl.ds(pl.multiple_of(b * TB, TB), TB)]

    def cut_res(b):
        for r in range(RHS):
            rpiece[r, pl.ds(b, 1), :] = res[pl.ds(r, 1), pl.ds(pl.multiple_of(b * TB, TB), TB)]

    repeat(PC, cut_dir, unroll=4)
    xg[i] = dpiece[...].astype(BF16)
    repeat(PR, cut_res, unroll=4)
    rg[j] = rpiece[...].astype(BF16)

    pl.semaphore_wait(barrier, 2 * (NG - 1))

    def send_x(d):
        return remote(xg.at[i], xg.at[i], x_ss.at[d], x_rs.at[d], row_peer(d + 1))

    def take_x(d):
        s = turn(i, -d - 1, NG)
        return remote(xg.at[s], xg.at[s], x_ss.at[d], x_rs.at[d], row_peer(d + 1))

    def z_send(buf, ss, rs, d):
        return remote(buf.at[j], buf.at[j], ss.at[d], rs.at[d], z_peer(d + 1))

    def z_take(buf, ss, rs, d):
        s = x * NZ + turn(z, -d - 1, NZ)
        return remote(buf.at[s], buf.at[s], ss.at[d], rs.at[d], z_peer(d + 1))

    def x_send(buf, ss, rs, e, d):
        s = x * NZ + turn(z, -e, NZ)
        return remote(buf.at[s], buf.at[s], ss.at[e, d], rs.at[e, d], x_peer(d + 1))

    def x_take(buf, ss, rs, e, d):
        s = turn(x, -d - 1, NX) * NZ + turn(z, -e, NZ)
        return remote(buf.at[s], buf.at[s], ss.at[e, d], rs.at[e, d], x_peer(d + 1))

    def gather_first(buf, zs, zr, xs, xr):
        repeat(NZ - 1, lambda d: z_send(buf, zs, zr, d).start())
        repeat(NX - 1, lambda d: x_send(buf, xs, xr, 0, d).start())

    def gather_forward(buf, zs, zr, xs, xr):
        def forward(d):
            z_take(buf, zs, zr, d).wait_recv()
            repeat(NX - 1, lambda f: x_send(buf, xs, xr, d + 1, f).start())

        repeat(NZ - 1, forward)

    def gather_last(buf, zs, zr, xs, xr):
        repeat(NZ, lambda e: repeat(NX - 1, lambda d: x_take(buf, xs, xr, e, d).wait_recv()))

    def gather_sent(buf, zs, zr, xs, xr):
        repeat(NZ - 1, lambda d: z_send(buf, zs, zr, d).wait_send())
        repeat(NZ, lambda e: repeat(NX - 1, lambda d: x_send(buf, xs, xr, e, d).wait_send()))

    repeat(NG - 1, lambda d: send_x(d).start())
    old = (rg, rz_ss, rz_rs, rx_ss, rx_rs)
    new = (ag, az_ss, az_rs, ax_ss, ax_rs)
    gather_first(*old)

    idx[...] = jnp.zeros_like(idx)
    idx[0:1, 0:K] = rows_v[0]
    idx[1:2, 0:K] = cols_v[0]
    count = count_s[0, 0]
    used = lax.broadcasted_iota(jnp.int32, (TB, KPAD), 1) < count
    down = lax.broadcasted_iota(jnp.int32, (TB, KPAD), 0)
    for c in range(BR // TB):
        hit = jnp.where((down + c * TB == idx[0:1, :]) & used, 1.0, 0.0).astype(BF16)
        hit_r[c * TB : (c + 1) * TB, 0:KPAD] = hit
        hit_r[c * TB : (c + 1) * TB, KPAD : 2 * KPAD] = hit
    for c in range(BC // TB):
        hit = jnp.where((down + c * TB == idx[1:2, :]) & used, 1.0, 0.0).astype(BF16)
        hit_c[c * TB : (c + 1) * TB, 0:KPAD] = hit
        hit_c[c * TB : (c + 1) * TB, KPAD : 2 * KPAD] = hit
    hilo[K:KPAD, :] = jnp.zeros((KPAD - K, RHS * TB), BF16)
    hilo[KPAD + K :, :] = jnp.zeros((KPAD - K, RHS * TB), BF16)

    top = lax.broadcasted_iota(jnp.int32, (8, TB), 0) < RHS
    slot = lax.broadcasted_iota(jnp.int32, (HALF, TB), 0)

    def spread(src, dst, p, blocks):
        at = pl.ds(pl.multiple_of(p * blocks, blocks), blocks)
        for r in range(RHS):
            v = src[p, r].astype(F32)
            dst[at, r, :] = v
            dst[at, RHS + r, :] = v

    def products(vec, index_s, transpose):
        axis = 0 if transpose else 1

        def pair(k):
            a = vec[index_s[0, 0, k]]
            b = vec[index_s[0, 0, k + HALF]]
            lhs = jnp.concatenate([jnp.where(top, a, 0.0), jnp.where(top, 0.0, b)], axis=1)
            rhs = jnp.concatenate([t[k], t[k + HALF]], axis=axis)
            ys[k] = lax.dot_general(
                lhs.astype(BF16), rhs, (((1,), (axis,)), ((), ())), preferred_element_type=F32
            )

        repeat(HALF, pair, unroll=8)
        for h in range(2):
            live = slot + h * HALF < count
            at = pl.ds(h * HALF, HALF)
            low_at = pl.ds(KPAD + h * HALF, HALF)
            for r in range(RHS):
                y = jnp.where(live, ys[:, h * RHS + r, :], 0.0)
                high = y.astype(BF16)
                hilo[at, r * TB : (r + 1) * TB] = high
                hilo[low_at, r * TB : (r + 1) * TB] = (y - high.astype(F32)).astype(BF16)

    def take_dir(d):
        take_x(d).wait_recv()
        spread(xg, xf, turn(i, -d - 1, NG), PC)

    spread(xg, xf, i, PC)
    repeat(NG - 1, take_dir)
    gather_forward(*old)
    for c in range(4):
        tile_copy(c).wait()
    products(xf, cols_s, False)

    def s1_send(d, e):
        p = turn(x, d + 1, NX) * NZ + turn(z, e + 1, NZ)
        dst = r1.at[turn(z, e + 1, NZ), x]
        return remote(sb.at[p], dst, s1_ss.at[d, e], s1_rs.at[d, e], x_peer(d + 1))

    def s1_take(d, e):
        dst = r1.at[turn(z, e + 1, NZ), turn(x, -d - 1, NX)]
        return remote(dst, dst, s1_ss.at[d, e], s1_rs.at[d, e], x_peer(d + 1))

    def s2_send(e):
        return remote(
            sb.at[x * NZ + turn(z, e + 1, NZ)], r2.at[z], s2_ss.at[e], s2_rs.at[e], z_peer(e + 1)
        )

    def s2_take(e):
        dst = r2.at[turn(z, -e - 1, NZ)]
        return remote(dst, dst, s2_ss.at[e], s2_rs.at[e], z_peer(e + 1))

    def image_chunk(d):
        xd = turn(x, d + 1, NX)
        hit = hit_r[pl.ds(pl.multiple_of(xd * TB, TB), TB), :]
        part = lax.dot_general(hit, hilo[...], (((1,), (0,)), ((), ())), preferred_element_type=F32)
        for q in range(NZ):
            for r in range(RHS):
                sb[xd * NZ + q, r] = part[q * PR : (q + 1) * PR, r * TB : (r + 1) * TB].astype(BF16)

    def image_out(d):
        image_chunk(d)
        repeat(NZ, lambda e: s1_send(d, e).start())

    repeat(NX - 1, image_out)
    image_chunk(NX - 1)

    spread(rg, rf, j, PR)

    def take_res(e):
        def one(d):
            x_take(*((rg,) + old[3:]), e, d).wait_recv()
            spread(rg, rf, turn(x, -d - 1, NX) * NZ + turn(z, -e, NZ), PR)

        repeat(NX - 1, one)

    repeat(NZ, take_res)
    repeat(NZ - 1, lambda d: spread(rg, rf, x * NZ + turn(z, -d - 1, NZ), PR))
    products(rf, rows_s, True)
    for c in range(BC // TB):
        grad_r[c * TB : (c + 1) * TB, :] = lax.dot_general(
            hit_c[c * TB : (c + 1) * TB, :], hilo[...], (((1,), (0,)), ((), ())),
            preferred_element_type=F32,
        )

    def over_x(e):
        zt = turn(z, e + 1, NZ)
        repeat(NX - 1, lambda d: s1_take(d, e).wait_recv())
        total = sb[x * NZ + zt].astype(F32)
        for d in range(NX - 1):
            total += r1[zt, turn(x, -d - 1, NX)].astype(F32)
        return total

    def through(e):
        sb[x * NZ + turn(z, e + 1, NZ)] = over_x(e).astype(BF16)
        s2_send(e).start()

    repeat(NZ - 1, through)
    image[...] = over_x(NZ - 1)

    def add_image(e):
        s2_take(e).wait_recv()
        image[...] += r2[turn(z, -e - 1, NZ)].astype(F32)

    repeat(NZ - 1, add_image)

    ag[j] = image[...].astype(BF16)
    gather_first(*new)

    def share(buf, me, peer, ss, rs):
        return lambda d: remote(buf.at[me], buf.at[me], ss.at[d], rs.at[d], peer(d + 1))

    def shared(buf, me, peer, ss, rs):
        def take(d):
            s = turn(me, -d - 1, NG)
            remote(buf.at[s], buf.at[s], ss.at[d], rs.at[d], peer(d + 1)).wait_recv()

        repeat(NG - 1, take)
        return jnp.sum(buf[...], axis=0)

    for r in range(RHS):
        v = image[r]
        ca[j, r : r + 1, :] = jnp.sum(v * v, axis=0, keepdims=True)
    c_col = (ca, j, col_peer, ca_ss, ca_rs)
    c_row = (cb, i, row_peer, cb_ss, cb_rs)
    repeat(NG - 1, lambda d: share(*c_col)(d).start())
    gather_forward(*new)
    cb[i] = shared(*c_col)
    repeat(NG - 1, lambda d: share(*c_row)(d).start())

    line = lax.broadcasted_iota(jnp.int32, (RHS, 1), 0)
    gamma = jnp.full((RHS, 1), gamma_s[0], F32)
    for r in range(1, RHS):
        gamma = jnp.where(line == r, gamma_s[r], gamma)

    curvature = jnp.sum(shared(*c_row)[0:RHS, :], axis=1, keepdims=True)
    step = gamma / curvature
    out_sol[...] = sol[...] + step * dirn[...]

    def write_res(b):
        for r in range(RHS):
            at = pl.ds(pl.multiple_of(b * TB, TB), TB)
            out_res[pl.ds(r, 1), at] = (
                res[pl.ds(r, 1), at] - step[r : r + 1, :] * image[r, pl.ds(b, 1), :]
            )

    repeat(PR, write_res, unroll=4)

    spread(ag, rf, j, PR)
    repeat(NZ - 1, lambda d: spread(ag, rf, x * NZ + turn(z, -d - 1, NZ), PR))

    def take_image(e):
        def one(d):
            x_take(*((ag,) + new[3:]), e, d).wait_recv()
            spread(ag, rf, turn(x, -d - 1, NX) * NZ + turn(z, -e, NZ), PR)

        repeat(NX - 1, one)

    repeat(NZ, take_image)
    products(rf, rows_s, True)

    def g_send(d):
        return remote(gs.at[turn(i, d + 1, NG)], gr.at[i], g_ss.at[d], g_rs.at[d], row_peer(d + 1))

    def g_take(d):
        dst = gr.at[turn(i, -d - 1, NG)]
        return remote(dst, dst, g_ss.at[d], g_rs.at[d], row_peer(d + 1))

    step_wide = jnp.concatenate(
        [jnp.broadcast_to(step[r : r + 1, :], (1, TB)) for r in range(RHS)], axis=1
    )
    for c in range(BC // TB):
        part = lax.dot_general(
            hit_c[c * TB : (c + 1) * TB, :], hilo[...], (((1,), (0,)), ((), ())),
            preferred_element_type=F32,
        )
        part = grad_r[c * TB : (c + 1) * TB, :] - step_wide * part
        for q in range(TB // PC):
            for r in range(RHS):
                gs[c * (TB // PC) + q, r] = part[
                    q * PC : (q + 1) * PC, r * TB : (r + 1) * TB
                ].astype(BF16)
    repeat(NG - 1, lambda d: g_send(d).start())

    repeat(NG - 1, lambda d: send_x(d).wait_send())
    gather_sent(*old)
    gather_sent(*new)
    repeat(NX - 1, lambda d: repeat(NZ, lambda e: s1_send(d, e).wait_send()))
    repeat(NZ - 1, lambda e: s2_send(e).wait_send())
    repeat(NG - 1, lambda d: share(*c_col)(d).wait_send())
    repeat(NG - 1, lambda d: share(*c_row)(d).wait_send())

    repeat(NG - 1, lambda d: g_take(d).wait_recv())
    gr[i] = gs[i]
    grad = gr[0].astype(F32)
    for s in range(1, NG):
        grad += gr[s].astype(F32)

    for r in range(RHS):
        v = grad[r]
        na[i, r : r + 1, :] = jnp.sum(v * v, axis=0, keepdims=True)
    n_row = (na, i, row_peer, na_ss, na_rs)
    n_col = (nb, j, col_peer, nb_ss, nb_rs)
    repeat(NG - 1, lambda d: share(*n_row)(d).start())
    nb[j] = shared(*n_row)
    repeat(NG - 1, lambda d: share(*n_col)(d).start())
    norm_next = jnp.sum(shared(*n_col)[0:RHS, :], axis=1, keepdims=True)
    beta = norm_next / gamma
    for r in range(RHS):
        full = grad[r] + beta[r : r + 1, :] * dpiece[r]
        for b in range(PC):
            out_dir[r : r + 1, b * TB : (b + 1) * TB] = full[b : b + 1, :]

    repeat(NG - 1, lambda d: g_send(d).wait_send())
    repeat(NG - 1, lambda d: share(*n_row)(d).wait_send())
    repeat(NG - 1, lambda d: share(*n_col)(d).wait_send())


def on_device(
    tile_values, tile_rows, tile_cols, tile_counts, solution, residual, direction, grad_norm
):
    smem = pl.BlockSpec(memory_space=pltpu.SMEM)
    vmem = pl.BlockSpec(memory_space=pltpu.VMEM)
    piece_r = (RHS, PR, TB)
    piece_c = (RHS, PC, TB)
    dma = pltpu.SemaphoreType.DMA
    peers = [dma((NG - 1,)), dma((NG - 1,))]
    staged = [dma((NZ - 1,)), dma((NZ - 1,)), dma((NZ, NX - 1)), dma((NZ, NX - 1))]
    return pl.pallas_call(
        kernel,
        out_shape=(
            jax.ShapeDtypeStruct(solution.shape, F32),
            jax.ShapeDtypeStruct(residual.shape, F32),
            jax.ShapeDtypeStruct(direction.shape, F32),
        ),
        in_specs=[smem, smem, smem, smem, vmem, vmem, pl.BlockSpec(memory_space=pltpu.HBM)]
        + [vmem] * 3,
        out_specs=(vmem, vmem, vmem),
        scratch_shapes=[
            pltpu.VMEM((K, TB, TB), BF16),
            pltpu.VMEM((NG,) + piece_c, BF16),
            pltpu.VMEM((NG,) + piece_r, BF16),
            pltpu.VMEM((NG,) + piece_r, BF16),
            pltpu.VMEM((NG,) + piece_r, BF16),
            pltpu.VMEM((NZ, NX) + piece_r, BF16),
            pltpu.VMEM((NZ,) + piece_r, BF16),
            pltpu.VMEM((NG,) + piece_c, BF16),
            pltpu.VMEM((NG,) + piece_c, BF16),
            pltpu.VMEM(piece_c, F32),
            pltpu.VMEM(piece_r, F32),
            pltpu.VMEM(piece_r, F32),
            pltpu.VMEM((BC, 2 * RHS, TB), F32),
            pltpu.VMEM((BR, 2 * RHS, TB), F32),
            pltpu.VMEM((HALF, 2 * RHS, TB), F32),
            pltpu.VMEM((2 * KPAD, RHS * TB), BF16),
            pltpu.VMEM((BR, 2 * KPAD), BF16),
            pltpu.VMEM((BC, 2 * KPAD), BF16),
            pltpu.VMEM((BC, RHS * TB), F32),
            pltpu.VMEM((8, KPAD), jnp.int32),
            pltpu.VMEM((NG, 8, TB), F32),
            pltpu.VMEM((NG, 8, TB), F32),
            pltpu.VMEM((NG, 8, TB), F32),
            pltpu.VMEM((NG, 8, TB), F32),
            dma((4,)),
            *peers,
            *staged,
            dma((NX - 1, NZ)), dma((NX - 1, NZ)),
            dma((NZ - 1,)), dma((NZ - 1,)),
            *staged,
            *peers,
            *peers, *peers, *peers, *peers,
        ],
        compiler_params=pltpu.CompilerParams(
            collective_id=0, has_side_effects=True, vmem_limit_bytes=60 * 1024 * 1024
        ),
    )(
        tile_counts, tile_rows, tile_cols, grad_norm, tile_rows, tile_cols,
        tile_values, solution, residual, direction,
    )


def solution(mesh):
    in_specs = (
        P("row", "col", None, None, None),
        P("row", "col", None),
        P("row", "col", None),
        P("row", "col"),
        P(None, ("col", "row")),
        P(None, ("row", "col")),
        P(None, ("col", "row")),
        P(),
    )
    out_specs = (P(None, ("col", "row")), P(None, ("row", "col")), P(None, ("col", "row")))
    return jax.shard_map(
        on_device, mesh=mesh, in_specs=in_specs, out_specs=out_specs, check_vma=False
    )
```

time: 784 us -> 82.3 us (0.10)
  waiting for transfers between devices: 482 us -> 0 us
  blocking collectives: 213 us -> 0 us
  Pallas kernels: 0 us -> 76.5 us
  local copies, waits for them, and re-layouts: 33.2 us -> 4.22 us
  other arithmetic: 27.9 us -> 0 us
  matrix products: 13.6 us -> 0 us
  between operations: 14.8 us -> 1.29 us
    unnamed x4 -> x0, waiting for transfers between devices: 482 us -> none
    psum x2 -> x0, blocking collectives: 155 us -> none  [the longest x1 77.4 us: on_device(): norm_next = lax.psum(jnp.sum(gradient * gradient, axis=1), ('row', 'col'))]
    pallas_call x0 -> x1, Pallas kernels: none -> 76.5 us  [on_device(): pl.pallas_call(kernel, out_shape=(jax.ShapeDtypeStruct(solution.shape, F3...]
    all_gather x2 -> x0, blocking collectives: 58.2 us -> none  [the longest x1 35.9 us: on_device(): lax.all_gather(new_residual.astype(jnp.bfloat16), 'col', axis=1, tiled=True)]
    unnamed x16 -> x3, local copies, waits for them, and re-layouts: 29 us -> 4.22 us
    scatter-add x2 -> x0, other arithmetic: 23.9 us -> none  [local_product(): summed = jax.ops.segment_sum(contrib, target, num_segments=blocks_out)]
    dot_general x2 -> x0, matrix products: 13.6 us -> none  [the longest x1 8.09 us: local_product(): jnp.einsum('kab,rkb->kra', tile_data, picked, preferred_element_type=jnp....]
  transfers between devices with their start and end apart: 2 -> 0, of which waited for: 2 -> 0; matrix products, arithmetic and copies ran while one was open for 0% -> 0% of each run, Pallas kernels for 0% -> 0%
where the time goes in v1:
time: 82.3 us; the launch traced here: 82 us
  Pallas kernels  76.5 us (93%)
  local copies, waits for them, and re-layouts  4.22 us (5%)
  between operations  1.29 us (2%)
    pallas_call x1, Pallas kernels, on_device(): pl.pallas_call(kernel, out_shape=(jax.ShapeDtypeStruct(solution.shape, F3...  76.5 us
    unnamed x3, local copies, waits for them, and re-layouts  4.22 us

profile of v1, /device:TPU:1, one launch (start us, length us, event | category | flops | bytes accessed | tf_op | source)
XLA Modules:
  0.0 82.0 jit_solution(9500636533584654715)
XLA Ops:
  1.3 76.5 %shard_map.103 = (f32[4,2048]{1,0:T(4,128)}, f32[4,4096]{1,0:T(4,128)}, f32[4,2048]{1,0:T(4,128)}) custom-call(s32[1,1]{1,0:T(1,128)S(6)} %copy.14.count_s, s32[1,1,320]{2,1,0:T(1,128)} %rows_v.1, s32[1,1,320]{2,1,0:T(1,128)} %cols_v.1, f32[4]{0:T(128)} %gamma_s.1, s32[1,1,320]{2,1,0:T(1,128)} %rows_v.1, s32[1,1,320]{2,1,0:T(1,128)} %cols_v.1, ...), custom_call_target="tpu_custom_call" | custom-call | tf_op jit(solution)/shard_map/pallas_call | solution.py:406
  77.8 1.4 %copy.15 = f32[4,2048]{1,0:T(4,128)} copy(f32[4,2048]{1,0:T(4,128)} %get-tuple-element.6) | data formatting | bytes 65536
  79.1 1.5 %copy.16 = f32[4,4096]{1,0:T(4,128)} copy(f32[4,4096]{1,0:T(4,128)} %get-tuple-element.7) | data formatting | bytes 131072
  80.6 1.4 %copy.17 = f32[4,2048]{1,0:T(4,128)} copy(f32[4,2048]{1,0:T(4,128)} %get-tuple-element.8) | data formatting | bytes 65536

commit v2 on v1

--- a/solution.py
+++ b/solution.py
@@ -11,10 +11,14 @@
 BC = 256
 K = 320
 HALF = K // 2
+QUARTER = K // 4
 KPAD = 384
 NG = 16
 NX = 4
 NZ = 4
+FAR_FIRST = (1, 0, 2)
+FAR_LAST = (0, 2, 1)
+NQ = NG // 2
 PR = BR // NG
 PC = BC // NG
 F32 = jnp.float32
@@ -46,17 +50,20 @@
 
 
 def kernel(
-    count_s, rows_s, cols_s, gamma_s, rows_v, cols_v, tiles, sol, res, dirn,
-    out_sol, out_res, out_dir,
+    count_s, rows_s, cols_s, gamma_s, rows_v, cols_v, tiles, res, dirn,
+    out_image, out_grad, out_scale,
     t, xg, ag, rg, sb, r1, r2, gs, gr, dpiece, rpiece, image, xf, rf, ys, hilo, hit_r, hit_c,
     grad_r, idx, ca, cb, na, nb,
-    t_sem, x_ss, x_rs, rz_ss, rz_rs, rx_ss, rx_rs, s1_ss, s1_rs, s2_ss, s2_rs,
+    t_sem, x_ss, x_rs, t_ss, t_rs, rz_ss, rz_rs, rx_ss, rx_rs, s1_ss, s1_rs, s2_ss, s2_rs,
     az_ss, az_rs, ax_ss, ax_rs, g_ss, g_rs, ca_ss, ca_rs, cb_ss, cb_rs, na_ss, na_rs, nb_ss, nb_rs,
 ):
     i = lax.axis_index("row")
     j = lax.axis_index("col")
     x = j // NZ
     z = lax.rem(j, NZ)
+    q = i // 2
+    core = lax.rem(i, 2)
+    twin = (q * 2 + 1 - core, j)
 
     def row_peer(d):
         return (turn(i, d, NG), j)
@@ -104,11 +111,20 @@
     pl.semaphore_wait(barrier, 2 * (NG - 1))
 
     def send_x(d):
-        return remote(xg.at[i], xg.at[i], x_ss.at[d], x_rs.at[d], row_peer(d + 1))
+        peer = (turn(q, d + 1, NQ) * 2 + core, j)
+        return remote(xg.at[i], xg.at[i], x_ss.at[d], x_rs.at[d], peer)
 
     def take_x(d):
-        s = turn(i, -d - 1, NG)
-        return remote(xg.at[s], xg.at[s], x_ss.at[d], x_rs.at[d], row_peer(d + 1))
+        s = turn(q, -d - 1, NQ) * 2 + core
+        return remote(xg.at[s], xg.at[s], x_ss.at[d], x_rs.at[d], twin)
+
+    def send_twin(d):
+        s = turn(q, -d, NQ) * 2 + core
+        return remote(xg.at[s], xg.at[s], t_ss.at[d], t_rs.at[d], twin)
+
+    def take_twin(d):
+        s = turn(q, -d, NQ) * 2 + 1 - core
+        return remote(xg.at[s], xg.at[s], t_ss.at[d], t_rs.at[d], twin)
 
     def z_send(buf, ss, rs, d):
         return remote(buf.at[j], buf.at[j], ss.at[d], rs.at[d], z_peer(d + 1))
@@ -126,24 +142,23 @@
         return remote(buf.at[s], buf.at[s], ss.at[e, d], rs.at[e, d], x_peer(d + 1))
 
     def gather_first(buf, zs, zr, xs, xr):
-        repeat(NZ - 1, lambda d: z_send(buf, zs, zr, d).start())
-        repeat(NX - 1, lambda d: x_send(buf, xs, xr, 0, d).start())
+        for d in FAR_FIRST:
+            z_send(buf, zs, zr, d).start()
+        for d in FAR_FIRST:
+            x_send(buf, xs, xr, 0, d).start()
 
     def gather_forward(buf, zs, zr, xs, xr):
-        def forward(d):
+        for d in FAR_LAST:
             z_take(buf, zs, zr, d).wait_recv()
-            repeat(NX - 1, lambda f: x_send(buf, xs, xr, d + 1, f).start())
-
-        repeat(NZ - 1, forward)
-
-    def gather_last(buf, zs, zr, xs, xr):
-        repeat(NZ, lambda e: repeat(NX - 1, lambda d: x_take(buf, xs, xr, e, d).wait_recv()))
+            for f in FAR_FIRST:
+                x_send(buf, xs, xr, d + 1, f).start()
 
     def gather_sent(buf, zs, zr, xs, xr):
         repeat(NZ - 1, lambda d: z_send(buf, zs, zr, d).wait_send())
         repeat(NZ, lambda e: repeat(NX - 1, lambda d: x_send(buf, xs, xr, e, d).wait_send()))
 
-    repeat(NG - 1, lambda d: send_x(d).start())
+    repeat(NQ - 1, lambda d: send_x(d).start())
+    send_twin(0).start()
     old = (rg, rz_ss, rz_rs, rx_ss, rx_rs)
     new = (ag, az_ss, az_rs, ax_ss, ax_rs)
     gather_first(*old)
@@ -178,16 +193,29 @@
     def products(vec, index_s, transpose):
         axis = 0 if transpose else 1
 
-        def pair(k):
-            a = vec[index_s[0, 0, k]]
-            b = vec[index_s[0, 0, k + HALF]]
-            lhs = jnp.concatenate([jnp.where(top, a, 0.0), jnp.where(top, 0.0, b)], axis=1)
-            rhs = jnp.concatenate([t[k], t[k + HALF]], axis=axis)
-            ys[k] = lax.dot_general(
+        def four(k):
+            v = [vec[index_s[0, 0, k + n * QUARTER]] for n in range(4)]
+            lhs = jnp.concatenate(
+                [
+                    jnp.concatenate([jnp.where(top, v[n], 0.0), jnp.where(top, 0.0, v[n + 2])], axis=1)
+                    for n in range(2)
+                ],
+                axis=0,
+            )
+            rhs = jnp.concatenate(
+                [
+                    jnp.concatenate([t[k + n * QUARTER], t[k + n * QUARTER + HALF]], axis=axis)
+                    for n in range(2)
+                ],
+                axis=1 - axis,
+            )
+            y = lax.dot_general(
                 lhs.astype(BF16), rhs, (((1,), (axis,)), ((), ())), preferred_element_type=F32
             )
-
-        repeat(HALF, pair, unroll=8)
+            ys[k] = y[0:8, 0:TB]
+            ys[k + QUARTER] = y[8:16, TB : 2 * TB]
+
+        repeat(QUARTER, four, unroll=40)
         for h in range(2):
             live = slot + h * HALF < count
             at = pl.ds(h * HALF, HALF)
@@ -200,11 +228,17 @@
 
     def take_dir(d):
         take_x(d).wait_recv()
-        spread(xg, xf, turn(i, -d - 1, NG), PC)
+        send_twin(d + 1).start()
+        spread(xg, xf, turn(q, -d - 1, NQ) * 2 + core, PC)
+
+    def take_other(d):
+        take_twin(d).wait_recv()
+        spread(xg, xf, turn(q, -d, NQ) * 2 + 1 - core, PC)
 
     spread(xg, xf, i, PC)
-    repeat(NG - 1, take_dir)
+    repeat(NQ - 1, take_dir)
     gather_forward(*old)
+    repeat(NQ, take_other)
     for c in range(4):
         tile_copy(c).wait()
     products(xf, cols_s, False)
@@ -235,11 +269,10 @@
             for r in range(RHS):
                 sb[xd * NZ + q, r] = part[q * PR : (q + 1) * PR, r * TB : (r + 1) * TB].astype(BF16)
 
-    def image_out(d):
-        image_chunk(d)
-        repeat(NZ, lambda e: s1_send(d, e).start())
-
-    repeat(NX - 1, image_out)
+    repeat(NX - 1, image_chunk)
+    for e in FAR_FIRST + (NZ - 1,):
+        for d in FAR_FIRST:
+            s1_send(d, e).start()
     image_chunk(NX - 1)
 
     spread(rg, rf, j, PR)
@@ -272,14 +305,16 @@
         sb[x * NZ + turn(z, e + 1, NZ)] = over_x(e).astype(BF16)
         s2_send(e).start()
 
-    repeat(NZ - 1, through)
+    for e in FAR_FIRST:
+        through(e)
     image[...] = over_x(NZ - 1)
 
     def add_image(e):
         s2_take(e).wait_recv()
         image[...] += r2[turn(z, -e - 1, NZ)].astype(F32)
 
-    repeat(NZ - 1, add_image)
+    for e in FAR_LAST:
+        add_image(e)
 
     ag[j] = image[...].astype(BF16)
     gather_first(*new)
@@ -305,24 +340,17 @@
     cb[i] = shared(*c_col)
     repeat(NG - 1, lambda d: share(*c_row)(d).start())
 
+    def write_image(b):
+        for r in range(RHS):
+            at = pl.ds(pl.multiple_of(b * TB, TB), TB)
+            out_image[pl.ds(r, 1), at] = image[r, pl.ds(b, 1), :]
+
+    repeat(PR, write_image, unroll=4)
     line = lax.broadcasted_iota(jnp.int32, (RHS, 1), 0)
     gamma = jnp.full((RHS, 1), gamma_s[0], F32)
     for r in range(1, RHS):
         gamma = jnp.where(line == r, gamma_s[r], gamma)
 
-    curvature = jnp.sum(shared(*c_row)[0:RHS, :], axis=1, keepdims=True)
-    step = gamma / curvature
-    out_sol[...] = sol[...] + step * dirn[...]
-
-    def write_res(b):
-        for r in range(RHS):
-            at = pl.ds(pl.multiple_of(b * TB, TB), TB)
-            out_res[pl.ds(r, 1), at] = (
-                res[pl.ds(r, 1), at] - step[r : r + 1, :] * image[r, pl.ds(b, 1), :]
-            )
-
-    repeat(PR, write_res, unroll=4)
-
     spread(ag, rf, j, PR)
     repeat(NZ - 1, lambda d: spread(ag, rf, x * NZ + turn(z, -d - 1, NZ), PR))
 
@@ -333,7 +361,8 @@
 
         repeat(NX - 1, one)
 
-    repeat(NZ, take_image)
+    for e in (0, 1, 3, 2):
+        take_image(e)
     products(rf, rows_s, True)
 
     def g_send(d):
@@ -343,6 +372,9 @@
         dst = gr.at[turn(i, -d - 1, NG)]
         return remote(dst, dst, g_ss.at[d], g_rs.at[d], row_peer(d + 1))
 
+    curvature = jnp.sum(shared(*c_row)[0:RHS, :], axis=1, keepdims=True)
+    step = gamma / curvature
+    out_scale[0] = jnp.broadcast_to(step, (RHS, TB))
     step_wide = jnp.concatenate(
         [jnp.broadcast_to(step[r : r + 1, :], (1, TB)) for r in range(RHS)], axis=1
     )
@@ -359,7 +391,8 @@
                 ].astype(BF16)
     repeat(NG - 1, lambda d: g_send(d).start())
 
-    repeat(NG - 1, lambda d: send_x(d).wait_send())
+    repeat(NQ - 1, lambda d: send_x(d).wait_send())
+    repeat(NQ, lambda d: send_twin(d).wait_send())
     gather_sent(*old)
     gather_sent(*new)
     repeat(NX - 1, lambda d: repeat(NZ, lambda e: s1_send(d, e).wait_send()))
@@ -379,18 +412,25 @@
     n_row = (na, i, row_peer, na_ss, na_rs)
     n_col = (nb, j, col_peer, nb_ss, nb_rs)
     repeat(NG - 1, lambda d: share(*n_row)(d).start())
+    for r in range(RHS):
+        for b in range(PC):
+            out_grad[r : r + 1, b * TB : (b + 1) * TB] = grad[r, b : b + 1, :]
     nb[j] = shared(*n_row)
     repeat(NG - 1, lambda d: share(*n_col)(d).start())
     norm_next = jnp.sum(shared(*n_col)[0:RHS, :], axis=1, keepdims=True)
-    beta = norm_next / gamma
-    for r in range(RHS):
-        full = grad[r] + beta[r : r + 1, :] * dpiece[r]
-        for b in range(PC):
-            out_dir[r : r + 1, b * TB : (b + 1) * TB] = full[b : b + 1, :]
+    out_scale[1] = jnp.broadcast_to(norm_next / gamma, (RHS, TB))
 
     repeat(NG - 1, lambda d: g_send(d).wait_send())
     repeat(NG - 1, lambda d: share(*n_row)(d).wait_send())
     repeat(NG - 1, lambda d: share(*n_col)(d).wait_send())
+
+
+def finish(sol, res, dirn, image, gradient, scale, out_sol, out_res, out_dir):
+    step = scale[0, :, 0:1]
+    beta = scale[1, :, 0:1]
+    out_sol[...] = sol[...] + step * dirn[...]
+    out_res[...] = res[...] - step * image[...]
+    out_dir[...] = gradient[...] + beta * dirn[...]
 
 
 def on_device(
@@ -403,15 +443,15 @@
     dma = pltpu.SemaphoreType.DMA
     peers = [dma((NG - 1,)), dma((NG - 1,))]
     staged = [dma((NZ - 1,)), dma((NZ - 1,)), dma((NZ, NX - 1)), dma((NZ, NX - 1))]
-    return pl.pallas_call(
+    image, gradient, scale = pl.pallas_call(
         kernel,
         out_shape=(
-            jax.ShapeDtypeStruct(solution.shape, F32),
             jax.ShapeDtypeStruct(residual.shape, F32),
             jax.ShapeDtypeStruct(direction.shape, F32),
+            jax.ShapeDtypeStruct((2, RHS, TB), F32),
         ),
         in_specs=[smem, smem, smem, smem, vmem, vmem, pl.BlockSpec(memory_space=pltpu.HBM)]
-        + [vmem] * 3,
+        + [vmem] * 2,
         out_specs=(vmem, vmem, vmem),
         scratch_shapes=[
             pltpu.VMEM((K, TB, TB), BF16),
@@ -439,7 +479,8 @@
             pltpu.VMEM((NG, 8, TB), F32),
             pltpu.VMEM((NG, 8, TB), F32),
             dma((4,)),
-            *peers,
+            dma((NQ - 1,)), dma((NQ - 1,)),
+            dma((NQ,)), dma((NQ,)),
             *staged,
             dma((NX - 1, NZ)), dma((NX - 1, NZ)),
             dma((NZ - 1,)), dma((NZ - 1,)),
@@ -452,8 +493,16 @@
         ),
     )(
         tile_counts, tile_rows, tile_cols, grad_norm, tile_rows, tile_cols,
-        tile_values, solution, residual, direction,
+        tile_values, residual, direction,
     )
+    return pl.pallas_call(
+        finish,
+        out_shape=tuple(
+            jax.ShapeDtypeStruct(a.shape, F32) for a in (solution, residual, direction)
+        ),
+        in_specs=[vmem] * 6,
+        out_specs=(vmem, vmem, vmem),
+    )(solution, residual, direction, image, gradient, scale)
 
 
 def solution(mesh):

time: 82.3 us -> 69.6 us (0.85)
  Pallas kernels: 76.5 us -> 68.1 us
  local copies, waits for them, and re-layouts: 4.22 us -> 0 us
    pallas_call x1 -> x2, Pallas kernels: 76.5 us -> 68.1 us  [the longest x1 66.5 us: on_device(): pl.pallas_call(kernel, out_shape=(jax.ShapeDtypeStruct(residual.shape, F3...]
    unnamed x3 -> x0, local copies, waits for them, and re-layouts: 4.22 us -> none
where the time goes in v2:
time: 69.6 us; the launch traced here: 69.4 us
  Pallas kernels  68.1 us (98%)
  between operations  1.29 us (2%)
    pallas_call x1, Pallas kernels, on_device(): pl.pallas_call(kernel, out_shape=(jax.ShapeDtypeStruct(residual.shape, F3...  66.5 us
    pallas_call x1, Pallas kernels, on_device(): pl.pallas_call(finish, out_shape=tuple((jax.ShapeDtypeStruct(a.shape, F32...  1.61 us

profile of v2, /device:TPU:1, one launch (start us, length us, event | category | flops | bytes accessed | tf_op | source)
XLA Modules:
  0.0 69.4 jit_solution(16048252838092878315)
XLA Ops:
  1.3 66.5 %shard_map.103 = (f32[4,4096]{1,0:T(4,128)}, f32[4,2048]{1,0:T(4,128)}, f32[2,4,128]{2,1,0:T(4,128)}) custom-call(s32[1,1]{1,0:T(1,128)S(6)} %copy.11.count_s, s32[1,1,320]{2,1,0:T(1,128)} %rows_v.1, s32[1,1,320]{2,1,0:T(1,128)} %cols_v.1, f32[4]{0:T(128)} %gamma_s.1, s32[1,1,320]{2,1,0:T(1,128)} %rows_v.1, s32[1,1,320]{2,1,0:T(1,128)} %cols_v.1, ...), custom_call_target="tpu_custom_call" | custom-call | tf_op jit(solution)/shard_map/pallas_call | solution.py:446
  67.8 1.6 %shard_map.104 = (f32[4,2048]{1,0:T(4,128)}, f32[4,4096]{1,0:T(4,128)}, f32[4,2048]{1,0:T(4,128)}) custom-call(f32[4,2048]{1,0:T(4,128)} %sol.1, f32[4,4096]{1,0:T(4,128)} %res.3, f32[4,2048]{1,0:T(4,128)} %dirn.3, f32[4,4096]{1,0:T(4,128)} %get-tuple-element.6.image, f32[4,2048]{1,0:T(4,128)} %get-tuple-element.7.gradient, f32[2,4,128]{2,1,0:T(4,128)} %get-tuple-element.8.scale), custom_call_target="tpu_custom_call" | custom-call | tf_op jit(solution)/shard_map/pallas_call | solution.py:498

commit v3 on v2

--- a/solution.py
+++ b/solution.py
@@ -52,10 +52,10 @@
 def kernel(
     count_s, rows_s, cols_s, gamma_s, rows_v, cols_v, tiles, res, dirn,
     out_image, out_grad, out_scale,
-    t, xg, ag, rg, sb, r1, r2, gs, gr, dpiece, rpiece, image, xf, rf, ys, hilo, hit_r, hit_c,
+    t, xg, ag, rg, sb, r1, r2, gs, gr, hs, hr, dpiece, rpiece, image, xf, rf, ys, hilo, hit_r, hit_c,
     grad_r, idx, ca, cb, na, nb,
-    t_sem, x_ss, x_rs, t_ss, t_rs, rz_ss, rz_rs, rx_ss, rx_rs, s1_ss, s1_rs, s2_ss, s2_rs,
-    az_ss, az_rs, ax_ss, ax_rs, g_ss, g_rs, ca_ss, ca_rs, cb_ss, cb_rs, na_ss, na_rs, nb_ss, nb_rs,
+    met, t_sem, x_ss, x_rs, t_ss, t_rs, rz_ss, rz_rs, rx_ss, rx_rs, s1_ss, s1_rs, s2_ss, s2_rs,
+    az_ss, az_rs, ax_ss, ax_rs, g_ss, g_rs, h_ss, h_rs, ca_ss, ca_rs, cb_ss, cb_rs, na_ss, na_rs, nb_ss, nb_rs,
 ):
     i = lax.axis_index("row")
     j = lax.axis_index("col")
@@ -89,11 +89,14 @@
 
     barrier = pltpu.get_barrier_semaphore()
 
-    def greet(d):
-        pl.semaphore_signal(barrier, inc=1, device_id=row_peer(d + 1), device_id_type=MESH)
-        pl.semaphore_signal(barrier, inc=1, device_id=col_peer(d + 1), device_id_type=MESH)
-
-    repeat(NG - 1, greet)
+    def greet(device):
+        pl.semaphore_signal(barrier, inc=1, device_id=device, device_id_type=MESH)
+
+    repeat(NG - 1, lambda d: greet(row_peer(d + 1)))
+    for d in FAR_FIRST:
+        greet(x_peer(d + 1))
+    for d in (0, 2):
+        greet(z_peer(d + 1))
 
     def cut_dir(b):
         for r in range(RHS):
@@ -108,7 +111,8 @@
     repeat(PR, cut_res, unroll=4)
     rg[j] = rpiece[...].astype(BF16)
 
-    pl.semaphore_wait(barrier, 2 * (NG - 1))
+    pl.semaphore_wait(barrier, NG - 1 + NX - 1 + 2)
+    pl.semaphore_signal(met, inc=1, device_id=z_peer(1), device_id_type=MESH)
 
     def send_x(d):
         peer = (turn(q, d + 1, NQ) * 2 + core, j)
@@ -161,6 +165,7 @@
     send_twin(0).start()
     old = (rg, rz_ss, rz_rs, rx_ss, rx_rs)
     new = (ag, az_ss, az_rs, ax_ss, ax_rs)
+    pl.semaphore_wait(met, 1)
     gather_first(*old)
 
     idx[...] = jnp.zeros_like(idx)
@@ -190,7 +195,7 @@
             dst[at, r, :] = v
             dst[at, RHS + r, :] = v
 
-    def products(vec, index_s, transpose):
+    def products(vec, index_s, transpose, between=None):
         axis = 0 if transpose else 1
 
         def four(k):
@@ -215,7 +220,11 @@
             ys[k] = y[0:8, 0:TB]
             ys[k + QUARTER] = y[8:16, TB : 2 * TB]
 
-        repeat(QUARTER, four, unroll=40)
+        half = QUARTER // 2
+        repeat(half, four, unroll=half)
+        if between is not None:
+            between()
+        repeat(half, lambda k: four(k + half), unroll=half)
         for h in range(2):
             live = slot + h * HALF < count
             at = pl.ds(h * HALF, HALF)
@@ -226,6 +235,35 @@
                 hilo[at, r * TB : (r + 1) * TB] = high
                 hilo[low_at, r * TB : (r + 1) * TB] = (y - high.astype(F32)).astype(BF16)
 
+    def grad_chunk(buf, c):
+        part = lax.dot_general(
+            hit_c[c * TB : (c + 1) * TB, :], hilo[...], (((1,), (0,)), ((), ())),
+            preferred_element_type=F32,
+        )
+        for n in range(TB // PC):
+            for r in range(RHS):
+                buf[c * (TB // PC) + n, r] = part[
+                    n * PC : (n + 1) * PC, r * TB : (r + 1) * TB
+                ].astype(BF16)
+
+    def g_send(src, dst, ss, rs, d):
+        return remote(src.at[turn(i, d + 1, NG)], dst.at[i], ss.at[d], rs.at[d], row_peer(d + 1))
+
+    def g_sum(src, dst, ss, rs):
+        def take(d):
+            slot = dst.at[turn(i, -d - 1, NG)]
+            remote(slot, slot, ss.at[d], rs.at[d], row_peer(d + 1)).wait_recv()
+
+        repeat(NG - 1, take)
+        dst[i] = src[i]
+        total = dst[0].astype(F32)
+        for n in range(1, NG):
+            total += dst[n].astype(F32)
+        return total
+
+    g_old = (hs, hr, h_ss, h_rs)
+    g_new = (gs, gr, g_ss, g_rs)
+
     def take_dir(d):
         take_x(d).wait_recv()
         send_twin(d + 1).start()
@@ -275,24 +313,6 @@
             s1_send(d, e).start()
     image_chunk(NX - 1)
 
-    spread(rg, rf, j, PR)
-
-    def take_res(e):
-        def one(d):
-            x_take(*((rg,) + old[3:]), e, d).wait_recv()
-            spread(rg, rf, turn(x, -d - 1, NX) * NZ + turn(z, -e, NZ), PR)
-
-        repeat(NX - 1, one)
-
-    repeat(NZ, take_res)
-    repeat(NZ - 1, lambda d: spread(rg, rf, x * NZ + turn(z, -d - 1, NZ), PR))
-    products(rf, rows_s, True)
-    for c in range(BC // TB):
-        grad_r[c * TB : (c + 1) * TB, :] = lax.dot_general(
-            hit_c[c * TB : (c + 1) * TB, :], hilo[...], (((1,), (0,)), ((), ())),
-            preferred_element_type=F32,
-        )
-
     def over_x(e):
         zt = turn(z, e + 1, NZ)
         repeat(NX - 1, lambda d: s1_take(d, e).wait_recv())
@@ -309,6 +329,21 @@
         through(e)
     image[...] = over_x(NZ - 1)
 
+    spread(rg, rf, j, PR)
+
+    def take_res(e):
+        def one(d):
+            x_take(*((rg,) + old[3:]), e, d).wait_recv()
+            spread(rg, rf, turn(x, -d - 1, NX) * NZ + turn(z, -e, NZ), PR)
+
+        repeat(NX - 1, one)
+
+    repeat(NZ, take_res)
+    repeat(NZ - 1, lambda d: spread(rg, rf, x * NZ + turn(z, -d - 1, NZ), PR))
+    products(rf, rows_s, True)
+    for c in range(BC // TB):
+        grad_chunk(hs, c)
+
     def add_image(e):
         s2_take(e).wait_recv()
         image[...] += r2[turn(z, -e - 1, NZ)].astype(F32)
@@ -337,6 +372,7 @@
     c_row = (cb, i, row_peer, cb_ss, cb_rs)
     repeat(NG - 1, lambda d: share(*c_col)(d).start())
     gather_forward(*new)
+    repeat(NG - 1, lambda d: g_send(*g_old, d).start())
     cb[i] = shared(*c_col)
     repeat(NG - 1, lambda d: share(*c_row)(d).start())
 
@@ -365,31 +401,9 @@
         take_image(e)
     products(rf, rows_s, True)
 
-    def g_send(d):
-        return remote(gs.at[turn(i, d + 1, NG)], gr.at[i], g_ss.at[d], g_rs.at[d], row_peer(d + 1))
-
-    def g_take(d):
-        dst = gr.at[turn(i, -d - 1, NG)]
-        return remote(dst, dst, g_ss.at[d], g_rs.at[d], row_peer(d + 1))
-
-    curvature = jnp.sum(shared(*c_row)[0:RHS, :], axis=1, keepdims=True)
-    step = gamma / curvature
-    out_scale[0] = jnp.broadcast_to(step, (RHS, TB))
-    step_wide = jnp.concatenate(
-        [jnp.broadcast_to(step[r : r + 1, :], (1, TB)) for r in range(RHS)], axis=1
-    )
     for c in range(BC // TB):
-        part = lax.dot_general(
-            hit_c[c * TB : (c + 1) * TB, :], hilo[...], (((1,), (0,)), ((), ())),
-            preferred_element_type=F32,
-        )
-        part = grad_r[c * TB : (c + 1) * TB, :] - step_wide * part
-        for q in range(TB // PC):
-            for r in range(RHS):
-                gs[c * (TB // PC) + q, r] = part[
-                    q * PC : (q + 1) * PC, r * TB : (r + 1) * TB
-                ].astype(BF16)
-    repeat(NG - 1, lambda d: g_send(d).start())
+        grad_chunk(gs, c)
+    repeat(NG - 1, lambda d: g_send(*g_new, d).start())
 
     repeat(NQ - 1, lambda d: send_x(d).wait_send())
     repeat(NQ, lambda d: send_twin(d).wait_send())
@@ -400,11 +414,12 @@
     repeat(NG - 1, lambda d: share(*c_col)(d).wait_send())
     repeat(NG - 1, lambda d: share(*c_row)(d).wait_send())
 
-    repeat(NG - 1, lambda d: g_take(d).wait_recv())
-    gr[i] = gs[i]
-    grad = gr[0].astype(F32)
-    for s in range(1, NG):
-        grad += gr[s].astype(F32)
+    grad_r[...] = g_sum(*g_old)
+    curvature = jnp.sum(shared(*c_row)[0:RHS, :], axis=1, keepdims=True)
+    step = gamma / curvature
+    out_scale[0] = jnp.broadcast_to(step, (RHS, TB))
+    total = g_sum(*g_new)
+    grad = [grad_r[r] - step[r : r + 1, :] * total[r] for r in range(RHS)]
 
     for r in range(RHS):
         v = grad[r]
@@ -414,13 +429,14 @@
     repeat(NG - 1, lambda d: share(*n_row)(d).start())
     for r in range(RHS):
         for b in range(PC):
-            out_grad[r : r + 1, b * TB : (b + 1) * TB] = grad[r, b : b + 1, :]
+            out_grad[r : r + 1, b * TB : (b + 1) * TB] = grad[r][b : b + 1, :]
     nb[j] = shared(*n_row)
     repeat(NG - 1, lambda d: share(*n_col)(d).start())
     norm_next = jnp.sum(shared(*n_col)[0:RHS, :], axis=1, keepdims=True)
     out_scale[1] = jnp.broadcast_to(norm_next / gamma, (RHS, TB))
 
-    repeat(NG - 1, lambda d: g_send(d).wait_send())
+    repeat(NG - 1, lambda d: g_send(*g_old, d).wait_send())
+    repeat(NG - 1, lambda d: g_send(*g_new, d).wait_send())
     repeat(NG - 1, lambda d: share(*n_row)(d).wait_send())
     repeat(NG - 1, lambda d: share(*n_col)(d).wait_send())
 
@@ -463,6 +479,8 @@
             pltpu.VMEM((NZ,) + piece_r, BF16),
             pltpu.VMEM((NG,) + piece_c, BF16),
             pltpu.VMEM((NG,) + piece_c, BF16),
+            pltpu.VMEM((NG,) + piece_c, BF16),
+            pltpu.VMEM((NG,) + piece_c, BF16),
             pltpu.VMEM(piece_c, F32),
             pltpu.VMEM(piece_r, F32),
             pltpu.VMEM(piece_r, F32),
@@ -472,12 +490,13 @@
             pltpu.VMEM((2 * KPAD, RHS * TB), BF16),
             pltpu.VMEM((BR, 2 * KPAD), BF16),
             pltpu.VMEM((BC, 2 * KPAD), BF16),
-            pltpu.VMEM((BC, RHS * TB), F32),
+            pltpu.VMEM(piece_c, F32),
             pltpu.VMEM((8, KPAD), jnp.int32),
             pltpu.VMEM((NG, 8, TB), F32),
             pltpu.VMEM((NG, 8, TB), F32),
             pltpu.VMEM((NG, 8, TB), F32),
             pltpu.VMEM((NG, 8, TB), F32),
+            pltpu.SemaphoreType.REGULAR,
             dma((4,)),
             dma((NQ - 1,)), dma((NQ - 1,)),
             dma((NQ,)), dma((NQ,)),
@@ -485,6 +504,7 @@
             dma((NX - 1, NZ)), dma((NX - 1, NZ)),
             dma((NZ - 1,)), dma((NZ - 1,)),
             *staged,
+            *peers,
             *peers,
             *peers, *peers, *peers, *peers,
         ],

time: 69.6 us -> 67 us (0.963)
  Pallas kernels: 68.1 us -> 65.5 us
    pallas_call x1, Pallas kernels: 66.5 us -> 63.9 us  [on_device(): pl.pallas_call(kernel, out_shape=(jax.ShapeDtypeStruct(residual.shape, F3...]
where the time goes in v3:
time: 67 us; the launch traced here: 66.8 us
  Pallas kernels  65.5 us (98%)
  between operations  1.29 us (2%)
    pallas_call x1, Pallas kernels, on_device(): pl.pallas_call(kernel, out_shape=(jax.ShapeDtypeStruct(residual.shape, F3...  63.9 us
    pallas_call x1, Pallas kernels, on_device(): pl.pallas_call(finish, out_shape=tuple((jax.ShapeDtypeStruct(a.shape, F32...  1.61 us

profile of v3, /device:TPU:1, one launch (start us, length us, event | category | flops | bytes accessed | tf_op | source)
XLA Modules:
  0.0 66.8 jit_solution(6362442125699372859)
XLA Ops:
  1.3 63.9 %shard_map.103 = (f32[4,4096]{1,0:T(4,128)}, f32[4,2048]{1,0:T(4,128)}, f32[2,4,128]{2,1,0:T(4,128)}) custom-call(s32[1,1]{1,0:T(1,128)S(6)} %copy.11.count_s, s32[1,1,320]{2,1,0:T(1,128)} %rows_v.1, s32[1,1,320]{2,1,0:T(1,128)} %cols_v.1, f32[4]{0:T(128)} %gamma_s.1, s32[1,1,320]{2,1,0:T(1,128)} %rows_v.1, s32[1,1,320]{2,1,0:T(1,128)} %cols_v.1, ...), custom_call_target="tpu_custom_call" | custom-call | tf_op jit(solution)/shard_map/pallas_call | solution.py:462
  65.2 1.6 %shard_map.104 = (f32[4,2048]{1,0:T(4,128)}, f32[4,4096]{1,0:T(4,128)}, f32[4,2048]{1,0:T(4,128)}) custom-call(f32[4,2048]{1,0:T(4,128)} %sol.1, f32[4,4096]{1,0:T(4,128)} %res.3, f32[4,2048]{1,0:T(4,128)} %dirn.3, f32[4,4096]{1,0:T(4,128)} %get-tuple-element.6.image, f32[4,2048]{1,0:T(4,128)} %get-tuple-element.7.gradient, f32[2,4,128]{2,1,0:T(4,128)} %get-tuple-element.8.scale), custom_call_target="tpu_custom_call" | custom-call | tf_op jit(solution)/shard_map/pallas_call | solution.py:518

commit v4 on v3

--- a/solution.py
+++ b/solution.py
@@ -41,12 +41,12 @@
     return lax.rem(base + step + size, size)
 
 
-def repeat(count, body, unroll=1):
+def repeat(count, body, unroll=16):
     def step(index, carry):
         body(index)
         return carry
 
-    lax.fori_loop(0, count, step, 0, unroll=unroll)
+    lax.fori_loop(0, count, step, 0, unroll=min(unroll, count))
 
 
 def kernel(
@@ -174,8 +174,9 @@
     count = count_s[0, 0]
     used = lax.broadcasted_iota(jnp.int32, (TB, KPAD), 1) < count
     down = lax.broadcasted_iota(jnp.int32, (TB, KPAD), 0)
+    piece_row = (down // PR) * (NZ * PR) + down % PR
     for c in range(BR // TB):
-        hit = jnp.where((down + c * TB == idx[0:1, :]) & used, 1.0, 0.0).astype(BF16)
+        hit = jnp.where((piece_row + c * PR == idx[0:1, :]) & used, 1.0, 0.0).astype(BF16)
         hit_r[c * TB : (c + 1) * TB, 0:KPAD] = hit
         hit_r[c * TB : (c + 1) * TB, KPAD : 2 * KPAD] = hit
     for c in range(BC // TB):
@@ -299,19 +300,18 @@
         dst = r2.at[turn(z, -e - 1, NZ)]
         return remote(dst, dst, s2_ss.at[e], s2_rs.at[e], z_peer(e + 1))
 
-    def image_chunk(d):
-        xd = turn(x, d + 1, NX)
-        hit = hit_r[pl.ds(pl.multiple_of(xd * TB, TB), TB), :]
+    def image_chunk(e):
+        ze = turn(z, e + 1, NZ)
+        hit = hit_r[pl.ds(pl.multiple_of(ze * TB, TB), TB), :]
         part = lax.dot_general(hit, hilo[...], (((1,), (0,)), ((), ())), preferred_element_type=F32)
-        for q in range(NZ):
+        for n in range(NX):
             for r in range(RHS):
-                sb[xd * NZ + q, r] = part[q * PR : (q + 1) * PR, r * TB : (r + 1) * TB].astype(BF16)
-
-    repeat(NX - 1, image_chunk)
+                sb[n * NZ + ze, r] = part[n * PR : (n + 1) * PR, r * TB : (r + 1) * TB].astype(BF16)
+
     for e in FAR_FIRST + (NZ - 1,):
+        image_chunk(e)
         for d in FAR_FIRST:
             s1_send(d, e).start()
-    image_chunk(NX - 1)
 
     def over_x(e):
         zt = turn(z, e + 1, NZ)
@@ -373,8 +373,6 @@
     repeat(NG - 1, lambda d: share(*c_col)(d).start())
     gather_forward(*new)
     repeat(NG - 1, lambda d: g_send(*g_old, d).start())
-    cb[i] = shared(*c_col)
-    repeat(NG - 1, lambda d: share(*c_row)(d).start())
 
     def write_image(b):
         for r in range(RHS):
@@ -397,22 +395,16 @@
 
         repeat(NX - 1, one)
 
-    for e in (0, 1, 3, 2):
+    for e in (0, 1, 3):
         take_image(e)
+    cb[i] = shared(*c_col)
+    repeat(NG - 1, lambda d: share(*c_row)(d).start())
+    take_image(2)
     products(rf, rows_s, True)
 
     for c in range(BC // TB):
         grad_chunk(gs, c)
     repeat(NG - 1, lambda d: g_send(*g_new, d).start())
-
-    repeat(NQ - 1, lambda d: send_x(d).wait_send())
-    repeat(NQ, lambda d: send_twin(d).wait_send())
-    gather_sent(*old)
-    gather_sent(*new)
-    repeat(NX - 1, lambda d: repeat(NZ, lambda e: s1_send(d, e).wait_send()))
-    repeat(NZ - 1, lambda e: s2_send(e).wait_send())
-    repeat(NG - 1, lambda d: share(*c_col)(d).wait_send())
-    repeat(NG - 1, lambda d: share(*c_row)(d).wait_send())
 
     grad_r[...] = g_sum(*g_old)
     curvature = jnp.sum(shared(*c_row)[0:RHS, :], axis=1, keepdims=True)
@@ -430,14 +422,22 @@
     for r in range(RHS):
         for b in range(PC):
             out_grad[r : r + 1, b * TB : (b + 1) * TB] = grad[r][b : b + 1, :]
+    repeat(NQ - 1, lambda d: send_x(d).wait_send())
+    repeat(NQ, lambda d: send_twin(d).wait_send())
+    gather_sent(*old)
+    repeat(NX - 1, lambda d: repeat(NZ, lambda e: s1_send(d, e).wait_send()))
+    repeat(NZ - 1, lambda e: s2_send(e).wait_send())
     nb[j] = shared(*n_row)
     repeat(NG - 1, lambda d: share(*n_col)(d).start())
-    norm_next = jnp.sum(shared(*n_col)[0:RHS, :], axis=1, keepdims=True)
-    out_scale[1] = jnp.broadcast_to(norm_next / gamma, (RHS, TB))
-
+    gather_sent(*new)
+    repeat(NG - 1, lambda d: share(*c_col)(d).wait_send())
+    repeat(NG - 1, lambda d: share(*c_row)(d).wait_send())
     repeat(NG - 1, lambda d: g_send(*g_old, d).wait_send())
     repeat(NG - 1, lambda d: g_send(*g_new, d).wait_send())
     repeat(NG - 1, lambda d: share(*n_row)(d).wait_send())
+    norm_next = jnp.sum(shared(*n_col)[0:RHS, :], axis=1, keepdims=True)
+    out_scale[1] = jnp.broadcast_to(norm_next / gamma, (RHS, TB))
+
     repeat(NG - 1, lambda d: share(*n_col)(d).wait_send())
 
 

time: 67 us -> 66.2 us (0.988)
  Pallas kernels: 65.5 us -> 64.7 us
    pallas_call x1, Pallas kernels: 63.9 us -> 63.1 us  [on_device(): pl.pallas_call(kernel, out_shape=(jax.ShapeDtypeStruct(residual.shape, F3...]
where the time goes in v4:
time: 66.2 us; the launch traced here: 66 us
  Pallas kernels  64.7 us (98%)
  between operations  1.29 us (2%)
    pallas_call x1, Pallas kernels, on_device(): pl.pallas_call(kernel, out_shape=(jax.ShapeDtypeStruct(residual.shape, F3...  63.1 us
    pallas_call x1, Pallas kernels, on_device(): pl.pallas_call(finish, out_shape=tuple((jax.ShapeDtypeStruct(a.shape, F32...  1.61 us

profile of v4, /device:TPU:1, one launch (start us, length us, event | category | flops | bytes accessed | tf_op | source)
XLA Modules:
  0.0 66.0 jit_solution(15596592842248307472)
XLA Ops:
  1.3 63.1 %shard_map.103 = (f32[4,4096]{1,0:T(4,128)}, f32[4,2048]{1,0:T(4,128)}, f32[2,4,128]{2,1,0:T(4,128)}) custom-call(s32[1,1]{1,0:T(1,128)S(6)} %copy.11.count_s, s32[1,1,320]{2,1,0:T(1,128)} %rows_v.1, s32[1,1,320]{2,1,0:T(1,128)} %cols_v.1, f32[4]{0:T(128)} %gamma_s.1, s32[1,1,320]{2,1,0:T(1,128)} %rows_v.1, s32[1,1,320]{2,1,0:T(1,128)} %cols_v.1, ...), custom_call_target="tpu_custom_call" | custom-call | tf_op jit(solution)/shard_map/pallas_call | solution.py:462
  64.4 1.6 %shard_map.104 = (f32[4,2048]{1,0:T(4,128)}, f32[4,4096]{1,0:T(4,128)}, f32[4,2048]{1,0:T(4,128)}) custom-call(f32[4,2048]{1,0:T(4,128)} %sol.1, f32[4,4096]{1,0:T(4,128)} %res.3, f32[4,2048]{1,0:T(4,128)} %dirn.3, f32[4,4096]{1,0:T(4,128)} %get-tuple-element.6.image, f32[4,2048]{1,0:T(4,128)} %get-tuple-element.7.gradient, f32[2,4,128]{2,1,0:T(4,128)} %get-tuple-element.8.scale), custom_call_target="tpu_custom_call" | custom-call | tf_op jit(solution)/shard_map/pallas_call | solution.py:518
